TPU v7x, 256 devices: a whole 4x4x8 slice. The times are simulated.
256 devices in a mesh: dp: 64 (over y, z, x_lo), mp: 4 (over x_hi, core).
Axes of the slice: x: 4 (x_hi: 2, x_lo: 2; x = x_hi * 2 + x_lo), y: 4, z: 8, core: 2. Of those that a mesh axis runs over, the one named last changes fastest.
Arguments:
- layer_input: bfloat16 [8192, 2560], P('dp'), may hold values from -16 to 16
- gate_weight: bfloat16 [2560, 7168], P('dp', 'mp'), may hold values from -0.125 to 0.125
- up_value: bfloat16 [8192, 7168], P('dp', 'mp'), may hold values from -6 to 6
- hidden_grad: bfloat16 [8192, 7168], P('dp', 'mp'), may hold values from -6 to 6
- sign_bits: int32 [7168], P('mp'), may hold values from 0 to 1
- scale_exponent: int32 [56], P('mp'), may hold values from 0 to 6
Outputs:
- input_grad: bfloat16 [8192, 2560], P(('dp', 'mp'))
- up_grad: bfloat16 [8192, 7168], P('dp', 'mp')
- weight_grad: float32 [2560, 7168], P('dp', 'mp')
All inputs are finite; a program needn't handle non-finite values.
Results may differ from a plain program's by a relative error of at most 0.0049.
Values may be sent and summed in bfloat16 or wider, within the bound.
A program may use at most 128 MiB of HBM per device.

v0:
```python
import math

import jax
import jax.numpy as jnp
from jax import lax
from jax.sharding import PartitionSpec as P


def hadamard_matrix():
    rows_index = lax.iota(jnp.int32, 128)
    both_bits = jnp.bitwise_and(rows_index[:, None], rows_index[None, :])
    parity = jnp.zeros((128, 128), jnp.int32)
    for bit_number in range(7):
        parity = parity + jnp.bitwise_and(jnp.right_shift(both_bits, bit_number), 1)
    signs = (1 - 2 * jnp.bitwise_and(parity, 1)).astype(jnp.float32)
    return signs / jnp.float32(math.sqrt(128.0))


def quantize(values, sign_values, hadamard, factors):
    row_total = values.shape[0]
    blocks = (values * sign_values).reshape(row_total, -1, 128)
    turned = jnp.einsum("rbk,kj->rbj", blocks, hadamard, precision=lax.Precision.HIGHEST)
    scaled = jnp.clip(turned * factors[None, :, None], -127.0, 127.0)
    return scaled.reshape(row_total, -1).astype(jnp.bfloat16)


def dequantize(values, sign_values, hadamard, factors):
    row_total = values.shape[0]
    blocks = values.reshape(row_total, -1, 128) / factors[None, :, None]
    turned = jnp.einsum("rbk,kj->rbj", blocks, hadamard, precision=lax.Precision.HIGHEST)
    return turned.reshape(row_total, -1) * sign_values


def local(layer_input, gate_weight, up_value, hidden_grad, sign_bits, scale_exponent):
    hadamard = hadamard_matrix()
    sign_values = (1 - 2 * sign_bits).astype(jnp.float32)
    factors = jnp.left_shift(jnp.ones_like(scale_exponent), scale_exponent).astype(jnp.float32)
    full_weight = lax.all_gather(gate_weight, "dp", axis=0, tiled=True)
    gate_value = jnp.dot(layer_input, full_weight, preferred_element_type=jnp.float32)
    sigmoid = jax.nn.sigmoid(gate_value)
    grad_float = hidden_grad.astype(jnp.float32)
    gate_grad = (
        grad_float * up_value.astype(jnp.float32) * sigmoid * (1.0 + gate_value * (1.0 - sigmoid))
    ).astype(jnp.bfloat16)
    up_grad = (grad_float * gate_value * sigmoid).astype(jnp.bfloat16)
    summed = lax.psum_scatter(
        lax.dot_general(
            gate_grad, full_weight, (((1,), (1,)), ((), ())), preferred_element_type=jnp.float32
        ),
        "mp",
        scatter_dimension=0,
        tiled=True,
    )
    input_grad = summed.astype(jnp.bfloat16)
    local_grad = lax.dot_general(
        layer_input, gate_grad, (((0,), (0,)), ((), ())), preferred_element_type=jnp.float32
    )
    quantized = quantize(local_grad, sign_values, hadamard, factors)
    summed = lax.psum_scatter(quantized.astype(jnp.float32), "dp", scatter_dimension=0, tiled=True)
    weight_grad = dequantize(summed, sign_values, hadamard, factors)
    return (input_grad, up_grad, weight_grad)


def solution(mesh):
    return jax.shard_map(
        local,
        mesh=mesh,
        in_specs=(P("dp", None), P("dp", "mp"), P("dp", "mp"), P("dp", "mp"), P("mp"), P("mp")),
        out_specs=(P(("dp", "mp"), None), P("dp", "mp"), P("dp", "mp")),
        check_vma=False,
    )
```

profile of v0, /device:TPU:8, one launch (start us, length us, event | category | flops | bytes accessed | tf_op | source)
XLA Modules:
  0.0 813.4 jit_solution(5157217649422387652)
XLA Ops:
  7.2 0.0 copy-start
  7.2 0.0 all-gather.2.cloned.1.call-start
  7.2 0.7 all-gather.2.cloned.1.call-update
  7.9 0.0 reduce-scatter.3.cloned.1.call-start
  8.0 0.7 shift-left_convert_fusion
  8.6 0.7 subtract_convert_fusion
  9.3 299.4 %all-gather.2.cloned.1.call-done = bf16[2560,1792]{1,0:T(8,128)(2,1)} async-done(((bf16[40,1792]{1,0:T(8,128)(2,1)}), bf16[2560,1792]{1,0:T(8,128)(2,1)}) %all-gather.2.cloned.1.call-update) | async-done | bytes 9175056 | tf_op jit(solution)/shard_map/all_gather | solution.py:38
  308.7 0.0 copy-done
  308.8 0.0 copy-start.2
  308.8 6.3 fusion.4
  315.1 0.1 copy-done.2
  315.2 4.1 fusion.24
  319.3 0.0 reduce-scatter.3.cloned.1.call-update
  319.4 0.0 reduce-scatter.5.cloned.1.call-start
  319.4 8.9 %convolution_multiply_fusion = f32[1792,2560]{1,0:T(8,128)} fusion(bf16[128,1792]{1,0:T(8,128)(2,1)S(1)} %get-tuple-element.4, bf16[128,2560]{1,0:T(8,128)(2,1)S(1)} %copy-done, f32[1792]{0:T(1024)S(1)} %subtract_convert_fusion), kind=kOutput, calls=%fused_computation.1 | convolution fusion | flops 1178992640 | bytes 19471360 | tf_op jit(solution)/shard_map/dot_general | solution.py:55
  328.3 24.6 %clamp_convert_fusion = bf16[2560,14,128]{0,2,1:T(8,128)(2,1)} fusion(f32[2560,14,128]{0,2,1:T(8,128)} %bitcast.23, f32[14]{0:T(128)S(1)} %shift-left_convert_fusion), kind=kOutput, calls=%fused_computation | convolution fusion | flops 7060619264 | bytes 27525176 | tf_op jit(solution)/shard_map/rbk,kj->rbj/dot_general | solution.py:22
  352.8 12.5 %bitcast_convert_fusion = f32[2560,1792]{0,1:T(8,128)} fusion(bf16[2560,14,128]{0,2,1:T(8,128)(2,1)} %clamp_convert_fusion), kind=kLoop, calls=%fused_computation.2 | loop fusion | flops 4587520 | bytes 27525120 | tf_op jit(solution)/shard_map/convert_element_type | solution.py:59
  365.4 0.0 copy-start.1
  365.4 19.4 %copy.13 = f32[2560,1792]{1,0:T(8,128)} copy(f32[2560,1792]{0,1:T(8,128)} %bitcast_convert_fusion) | data formatting | bytes 36700160 | tf_op jit(solution)/shard_map/convert_element_type | solution.py:59
  384.8 0.0 reduce-scatter.5.cloned.1.call-update
  384.8 0.0 reduce-scatter.3.cloned.1.call-done
  384.8 1.7 convert_element_type.39
  386.5 418.0 %reduce-scatter.5.cloned.1.call-done = f32[40,1792]{1,0:T(8,128)} async-done(((f32[2560,1792]{1,0:T(8,128)}), f32[40,1792]{1,0:T(8,128)}) %reduce-scatter.5.cloned.1.call-update) | async-done | bytes 286736 | tf_op jit(solution)/shard_map/reduce_scatter | solution.py:59
  804.5 1.0 reshape.22
  805.6 0.1 broadcast_divide_fusion
  805.7 0.5 convolution_bitcast_fusion
  806.1 0.7 bitcast_multiply_fusion
  806.9 0.0 copy-done.1
Async XLA Ops:
  7.2 301.6 %copy-start = (bf16[128,2560]{1,0:T(8,128)(2,1)S(1)}, bf16[128,2560]{1,0:T(8,128)(2,1)}, u32[]{:S(2)}) copy-start(bf16[128,2560]{1,0:T(8,128)(2,1)} %param.6) | copy-start | bytes 1966084
  7.2 301.6 %all-gather.2.cloned.1.call-start = ((), (), s32[]{:S(2)}) async-start(), calls=%async_computation.2 | async-start | bytes 9318400 | tf_op jit(solution)/shard_map/all_gather | solution.py:38
  7.9 376.9 %reduce-scatter.3.cloned.1.call-start = ((), (), s32[]{:S(2)}) async-start(), calls=%async_computation.3 | async-start | bytes 1638400 | tf_op jit(solution)/shard_map/reduce_scatter | solution.py:46
  308.8 6.5 copy-start.2
  319.4 485.2 %reduce-scatter.5.cloned.1.call-start = ((), (), s32[]{:S(2)}) async-start(), calls=%async_computation.4 | async-start | bytes 18636800 | tf_op jit(solution)/shard_map/reduce_scatter | solution.py:59
  365.4 441.5 %copy-start.1 = (bf16[128,2560]{1,0:T(8,128)(2,1)S(1)}, bf16[128,2560]{1,0:T(8,128)(2,1)}, u32[]{:S(2)}) copy-start(bf16[128,2560]{1,0:T(8,128)(2,1)} %param.6) | copy-start | bytes 1966084
Sparse Core Ops, SparseCore 0:
  9.8 298.8 all-gather.1
  319.5 55.6 reduce-scatter.2
  384.9 419.5 reduce-scatter.4
where the time goes:
time: 817 us; the launch traced here: 813 us
  waiting for transfers between devices  718 us (88%)
  matrix products  44.3 us (5%)
  local copies, waits for them, and re-layouts  20.6 us (3%)
  other arithmetic  16.4 us (2%)
  between operations  13.8 us (2%)
    reduce_scatter x1, waiting for transfers between devices, local(): lax.psum_scatter(quantized.astype(jnp.float32), 'dp', scatter_dimension=0...  418 us
    all_gather x1, waiting for transfers between devices, local(): full_weight = lax.all_gather(gate_weight, 'dp', axis=0, tiled=True)  299 us
    dot_general x1, matrix products, quantize(): jnp.einsum('rbk,kj->rbj', blocks, hadamard, precision=lax.Precision.HIGHEST)  24.6 us
    convert_element_type x1, local copies, waits for them, and re-layouts, local(): quantized.astype(jnp.float32)  19.4 us
  transfers between devices with their start and end apart: 3, of which 2 were waited for; matrix products, arithmetic and copies ran while one was open for 8% of the time, Pallas kernels for 0%

commit v1 on v0

v1 whole, which is shorter than its diff:
```python
import functools
import math

import jax
import jax.numpy as jnp
from jax import lax
from jax.experimental import pallas as pl
from jax.experimental.pallas import tpu as pltpu
from jax.sharding import PartitionSpec as P

F32 = jnp.float32
BF16 = jnp.bfloat16
MESH = pl.DeviceIdType.MESH
BLOCK = 128
ROOT = 1.0 / math.sqrt(128.0)


def up_to(value, unit):
    return -(-value // unit) * unit


class Dims:
    def __init__(self, ny, nz, tokens, depth, rows, hidden):
        self.ny, self.nz = ny, nz
        self.tokens, self.depth, self.rows, self.hidden = tokens, depth, rows, hidden
        self.half = hidden // 2
        self.blocks = self.half // BLOCK
        self.cols_a = (self.blocks * 3 // 7) * BLOCK
        self.cols_b = self.half - self.cols_a
        self.rb = 2 * rows
        self.yrows = nz * self.rb
        self.pad = up_to(rows, 16)
        cut = up_to(self.rb // 2, 16)
        self.row_subs = ((0, cut), (cut, self.rb - cut))
        quarter = self.yrows // 4
        self.y_subs = tuple((s * quarter, quarter) for s in range(4))


class Ring:
    def __init__(self, me, length, at):
        self.me, self.length, self.half = me, length, length // 2
        self.sides = (at(lax.rem(me + 1, length)), at(lax.rem(me + length - 1, length)))

    def place(self, offset):
        return lax.rem(self.me + offset + self.length, self.length)


class Sends:
    def __init__(self):
        self.open = []

    def start(self, src, dst, send_sem, recv_sem, device):
        copy = pltpu.make_async_remote_copy(
            src_ref=src, dst_ref=dst, send_sem=send_sem, recv_sem=recv_sem,
            device_id=device, device_id_type=MESH,
        )
        copy.start()
        self.open.append(copy)

    def drain(self):
        for copy in self.open:
            copy.wait_send()
        self.open = []


def went(side, sub, count):
    return (sub < (count + 1) // 2) == (side == 0)


class Gather:
    def __init__(self, ring, count, ref, sems, sends):
        self.ring, self.count, self.ref = ring, count, ref
        self.send_sems, self.recv_sems = sems
        self.sends = sends

    def wait_one(self, side, step, sub):
        origin = self.ring.place(-step if side == 0 else step)
        here = self.ref(origin, sub)
        pltpu.make_async_remote_copy(
            src_ref=here, dst_ref=here,
            send_sem=self.send_sems.at[side, step - 1, sub],
            recv_sem=self.recv_sems.at[side, step - 1, sub],
            device_id=self.ring.sides[side], device_id_type=MESH,
        ).wait_recv()

    def send(self, step):
        last = step == self.ring.half
        for sub in range(self.count):
            for side in (0, 1):
                if step > 1:
                    self.wait_one(side, step - 1, sub)
                if last and not went(side, sub, self.count):
                    continue
                origin = self.ring.place(-(step - 1) if side == 0 else step - 1)
                here = self.ref(origin, sub)
                self.sends.start(
                    here, here,
                    self.send_sems.at[side, step - 1, sub],
                    self.recv_sems.at[side, step - 1, sub],
                    self.ring.sides[side],
                )

    def finish(self):
        for sub in range(self.count):
            for side in (0, 1):
                if went(side, sub, self.count):
                    self.wait_one(side, self.ring.half, sub)


class Scatter:
    def __init__(self, ring, count, own, out, landing, sems, sends):
        self.ring, self.count, self.own, self.out, self.landing = ring, count, own, out, landing
        self.send_sems, self.recv_sems = sems
        self.sends = sends

    def arrived(self, side, step, sub):
        return step < 1 or step > 1 or went(side, sub, self.count)

    def take(self, side, step, sub):
        here = self.landing(side, step - 1, sub)
        pltpu.make_async_remote_copy(
            src_ref=here, dst_ref=here,
            send_sem=self.send_sems.at[side, step - 1, sub],
            recv_sem=self.recv_sems.at[side, step - 1, sub],
            device_id=self.ring.sides[side], device_id_type=MESH,
        ).wait_recv()
        return here[...].astype(F32)

    def send(self, step):
        far = self.ring.half + 1 - step
        for sub in range(self.count):
            for side in (0, 1):
                if step == 1 and not went(side, sub, self.count):
                    continue
                target = self.ring.place(far if side == 0 else -far)
                total = self.own(target, sub)[...]
                if step > 1 and self.arrived(side, step - 1, sub):
                    total = total + self.take(side, step - 1, sub)
                out = self.out(target, sub)
                out[...] = total.astype(BF16)
                self.sends.start(
                    out, self.landing(side, step - 1, sub),
                    self.send_sems.at[side, step - 1, sub],
                    self.recv_sems.at[side, step - 1, sub],
                    self.ring.sides[side],
                )

    def finish(self):
        for sub in range(self.count):
            mine = self.own(self.ring.me, sub)
            total = mine[...]
            for side in (0, 1):
                if self.arrived(side, self.ring.half, sub):
                    total = total + self.take(side, self.ring.half, sub)
            mine[...] = total


def hadamard_signs():
    both = jnp.bitwise_and(
        lax.broadcasted_iota(jnp.int32, (BLOCK, BLOCK), 0),
        lax.broadcasted_iota(jnp.int32, (BLOCK, BLOCK), 1),
    )
    for shift in (4, 2, 1):
        both = jnp.bitwise_xor(both, jnp.right_shift(both, shift))
    return (1 - 2 * jnp.bitwise_and(both, 1)).astype(F32).astype(BF16)


def kernel(
    dims,
    x_ref, w_ref, up_ref, hg_ref, bits_ref, exp_ref,
    ig_ref, ug_ref, wg_ref,
    x2, xt, hg2, up2, upg2, wsend, wrecv, wa, wb, g_a, g_b, turned, had,
    sa, sb, oa, ob, la_z, la_y, lb_y, lb_z,
    part, core_out, core_in, chip_out, chip_in,
    x_sems, core_sems, ip_sems, fin_sems, local_sem,
    ga_y_s, ga_y_r, ga_z_s, ga_z_r, gb_z_s, gb_z_r, gb_y_s, gb_y_r,
    ra_z_s, ra_z_r, ra_y_s, ra_y_r, rb_y_s, rb_y_r, rb_z_s, rb_z_r,
):
    d = dims
    t, hf, rb = d.tokens, d.half, d.rb
    dp, mp = lax.axis_index("dp"), lax.axis_index("mp")
    xl, yz = lax.rem(dp, 2), lax.div(dp, 2)
    z, y = lax.rem(yz, d.nz), lax.div(yz, d.nz)
    core, xh = lax.rem(mp, 2), lax.div(mp, 2)

    def device(y=y, z=z, xl=xl, xh=xh, core=core):
        return {"dp": (y * d.nz + z) * 2 + xl, "mp": xh * 2 + core}

    ring_y = Ring(y, d.ny, lambda place: device(y=place))
    ring_z = Ring(z, d.nz, lambda place: device(z=place))
    partner, sibling = device(xl=1 - xl), device(core=1 - core)
    across = (partner, device(xh=1 - xh), device(xl=1 - xl, xh=1 - xh))

    barrier = pltpu.get_barrier_semaphore()
    others = ring_y.sides + ring_z.sides + across + (sibling,)
    for other in others:
        pl.semaphore_signal(barrier, inc=1, device_id=other, device_id_type=MESH)

    sends = Sends()
    here = pl.ds(pl.multiple_of(xl * hf, BLOCK), hf)
    there = pl.ds(pl.multiple_of((1 - xl) * hf, BLOCK), hf)

    def padded(columns):
        rows = w_ref[:, columns].astype(F32)
        if d.pad == d.rows:
            return rows
        return jnp.concatenate([rows, jnp.zeros((d.pad - d.rows, hf), F32)], axis=0)

    wsend[...] = padded(there).astype(BF16)
    pl.semaphore_wait(barrier, len(others))

    sends.start(wsend, wrecv, x_sems.at[0, 0], x_sems.at[1, 0], partner)
    x_rows = pl.ds(pl.multiple_of(core * (t // 2), 16), t // 2)
    sends.start(x_ref.at[x_rows, :], x2.at[xl, x_rows, :], x_sems.at[0, 1], x_sems.at[1, 1], partner)
    sends.start(hg_ref.at[:, there], hg2.at[xl], x_sems.at[0, 2], x_sems.at[1, 2], partner)
    sends.start(up_ref.at[:, there], up2.at[xl], x_sems.at[0, 3], x_sems.at[1, 3], partner)
    own_x = pltpu.make_async_copy(x_ref, x2.at[xl], local_sem)
    own_x.start()

    def landed(ref, index):
        pltpu.make_async_remote_copy(
            src_ref=ref, dst_ref=ref, send_sem=x_sems.at[0, index], recv_sem=x_sems.at[1, index],
            device_id=partner, device_id_type=MESH,
        ).wait_recv()

    z_rows = lambda place: pl.multiple_of(place * rb, 16)
    ra = lambda ref: lambda place, sub: ref.at[place, pl.ds(z_rows(z) + d.row_subs[sub][0], d.row_subs[sub][1]), :]
    rz = lambda ref: lambda place, sub: ref.at[sub, pl.ds(z_rows(place), rb), :]
    rbz = lambda ref: lambda place, sub: ref.at[y, pl.ds(z_rows(place) + d.row_subs[sub][0], d.row_subs[sub][1]), :]
    rby = lambda ref: lambda place, sub: ref.at[place, pl.ds(d.y_subs[sub][0], d.y_subs[sub][1]), :]

    gather_a_y = Gather(ring_y, 2, ra(wa), (ga_y_s, ga_y_r), sends)
    gather_a_z = Gather(ring_z, d.ny, rz(wa), (ga_z_s, ga_z_r), sends)
    gather_b_z = Gather(ring_z, 2, rbz(wb), (gb_z_s, gb_z_r), sends)
    gather_b_y = Gather(ring_y, 4, rby(wb), (gb_y_s, gb_y_r), sends)

    landed(wrecv, 0)
    own_rows = w_ref[:, here].astype(F32)
    other_rows = wrecv[...].astype(F32)[: d.rows]
    low = jnp.where(xl == 0, own_rows, other_rows)
    high = jnp.where(xl == 0, other_rows, own_rows)
    rows = jnp.concatenate([low, high], axis=0).astype(BF16)
    wa[y, pl.ds(z_rows(z), rb), :] = rows[:, : d.cols_a]
    wb[y, pl.ds(z_rows(z), rb), :] = rows[:, d.cols_a :]

    gather_a_y.send(1)
    gather_b_z.send(1)
    had[...] = hadamard_signs()
    for step in range(2, d.ny // 2 + 1):
        gather_a_y.send(step)
    gather_a_y.finish()
    gather_a_z.send(1)
    for step in range(2, d.nz // 2 + 1):
        gather_b_z.send(step)
    gather_b_z.finish()
    gather_b_y.send(1)

    own_x.wait()
    theirs = x2.at[1 - xl, x_rows, :]
    landed(theirs, 1)
    sends.start(theirs, theirs, core_sems.at[0, 0], core_sems.at[1, 0], sibling)

    per_y = d.yrows // BLOCK

    def turn(replica):
        @pl.loop(0, d.depth // BLOCK)
        def _(chunk):
            tile = x2[replica, :, pl.ds(pl.multiple_of(chunk * BLOCK, BLOCK), BLOCK)]
            tile = tile.astype(F32).T.astype(BF16)
            at = pl.ds(pl.multiple_of(lax.rem(chunk, per_y) * BLOCK, BLOCK), BLOCK)
            xt[replica, lax.div(chunk, per_y), at, 0:t] = tile
            xt[replica, lax.div(chunk, per_y), at, t : 2 * t] = tile

    turn(xl)
    for step in range(2, d.nz // 2 + 1):
        gather_a_z.send(step)
        if step == 2:
            other_x = pl.ds(pl.multiple_of((1 - core) * (t // 2), 16), t // 2)
            rest = x2.at[1 - xl, other_x, :]
            pltpu.make_async_remote_copy(
                src_ref=rest, dst_ref=rest, send_sem=core_sems.at[0, 0], recv_sem=core_sems.at[1, 0],
                device_id=sibling, device_id_type=MESH,
            ).wait_recv()
    turn(1 - xl)
    for step in range(2, d.ny // 2 + 1):
        gather_b_y.send(step)
    landed(hg2.at[1 - xl], 2)
    landed(up2.at[1 - xl], 3)
    hg2[xl] = hg_ref[:, here]
    up2[xl] = up_ref[:, here]
    gather_a_z.finish()
    gather_b_y.finish()

    def scale_of(block):
        return jnp.left_shift(1, exp_ref[xl * d.blocks + block]).astype(F32)

    def inverse_of(block):
        return jnp.right_shift(64, exp_ref[xl * d.blocks + block]).astype(F32) * (1.0 / 64.0)

    def signs_of(block):
        bits = bits_ref[:, pl.ds(pl.multiple_of(xl * hf + block * BLOCK, BLOCK), BLOCK)]
        return (1 - 2 * bits).astype(F32)

    def gate_tile(w_part, g_part, base, start, width):
        columns = slice(start, start + width)
        gate = jnp.zeros((2 * t, width), F32)
        for place in range(d.ny):
            at = slice(place * d.yrows, (place + 1) * d.yrows)
            gate = gate + jnp.dot(
                x2[:, :, at].reshape(2 * t, d.yrows), w_part[place, :, columns],
                preferred_element_type=F32,
            )
        at = slice(base + start, base + start + width)
        grad = hg2[:, :, at].reshape(2 * t, width).astype(F32)
        up = up2[:, :, at].reshape(2 * t, width).astype(F32)
        s = jax.nn.sigmoid(gate)
        gate_grad = (grad * up * s * (1.0 + gate * (1.0 - s))).astype(BF16)
        g_part[:, columns] = gate_grad
        upg2[:, :, at] = (grad * gate * s).astype(BF16).reshape(2, t, width)
        for piece in range(width // BLOCK):
            block = (base + start) // BLOCK + piece
            flipped = gate_grad[:, piece * BLOCK : (piece + 1) * BLOCK].astype(F32) * signs_of(block)
            rotated = jnp.dot(flipped.astype(BF16), had[...], preferred_element_type=F32)
            rotated = rotated * (scale_of(block) * ROOT)
            top = rotated.astype(BF16)
            rest = (rotated - top.astype(F32)).astype(BF16)
            put = slice(block * BLOCK, (block + 1) * BLOCK)
            for replica in (0, 1):
                mine = slice(replica * t, (replica + 1) * t)
                turned[replica, 0:t, put] = top[mine]
                turned[replica, t : 2 * t, put] = rest[mine]

    for start in range(0, d.cols_b, 2 * BLOCK):
        gate_tile(wb, g_b, d.cols_a, start, min(2 * BLOCK, d.cols_b - start))
    for start in range(0, d.cols_a, 2 * BLOCK):
        gate_tile(wa, g_a, 0, start, min(2 * BLOCK, d.cols_a - start))

    sends.start(upg2.at[1 - xl], ug_ref.at[:, here], x_sems.at[0, 4], x_sems.at[1, 4], partner)
    ug_ref[:, here] = upg2[xl]

    def quantized(lhs, replica, columns):
        value = jnp.dot(lhs, turned[replica, :, columns], preferred_element_type=F32)
        return jnp.clip(value, -127.0, 127.0).astype(BF16).astype(F32)

    def order(j, ring):
        return ring.place((ring.half - lax.div(j + 1, 2)) * (2 * lax.rem(j, 2) - 1))

    def grads_a(low, high):
        @pl.loop(low, high)
        def _(j):
            at = pl.ds(z_rows(order(j, ring_z)), rb)
            total = 0.0
            for replica in (0, 1):
                lhs = xt[replica, :, at, :].reshape(d.ny * rb, 2 * t)
                total = total + quantized(lhs, replica, slice(0, d.cols_a))
            sa[:, at, :] = total.reshape(d.ny, rb, d.cols_a)

    def grads_b(low, high):
        @pl.loop(low * 2, high * 2)
        def _(j):
            place = order(lax.div(j, 2), ring_y)
            at = pl.ds(pl.multiple_of(lax.rem(j, 2) * (d.yrows // 2), 16), d.yrows // 2)
            total = 0.0
            for replica in (0, 1):
                total = total + quantized(xt[replica, place, at, :], replica, slice(d.cols_a, hf))
            sb[place, at, :] = total

    at_sub = lambda ref: lambda side, step, sub: ref.at[side, step, sub]
    at_rows = lambda ref: lambda side, step, sub: ref.at[side, step, pl.ds(d.row_subs[sub][0], d.row_subs[sub][1]), :]
    at_y = lambda ref: lambda side, step, sub: ref.at[side, step, pl.ds(d.y_subs[sub][0], d.y_subs[sub][1]), :]
    scatter_a_z = Scatter(ring_z, d.ny, rz(sa), rz(oa), at_sub(la_z), (ra_z_s, ra_z_r), sends)
    scatter_a_y = Scatter(ring_y, 2, ra(sa), ra(oa), at_rows(la_y), (ra_y_s, ra_y_r), sends)
    scatter_b_y = Scatter(ring_y, 4, rby(sb), rby(ob), at_y(lb_y), (rb_y_s, rb_y_r), sends)
    scatter_b_z = Scatter(ring_z, 2, rbz(sb), rbz(ob), at_rows(lb_z), (rb_z_s, rb_z_r), sends)

    grads_b(0, 1)
    scatter_b_y.send(1)
    grads_a(0, 1)
    scatter_a_z.send(1)
    grads_a(1, d.nz)
    grads_b(1, d.ny)

    def partial_tile(place):
        total = 0.0
        for w_part, g_part in ((wa, g_a), (wb, g_b)):
            total = total + lax.dot_general(
                g_part[...], w_part[place], (((1,), (1,)), ((), ())), preferred_element_type=F32
            )
        return total.reshape(8, t // 4, d.yrows)

    @pl.loop(0, d.ny)
    def _(place):
        part[:, :, pl.ds(pl.multiple_of(place * d.yrows, BLOCK), d.yrows)] = partial_tile(place)

    @pl.loop(0, 4)
    def _(q):
        core_out[q] = part[2 * q + 1 - core].astype(BF16)

    sends.start(core_out, core_in, core_sems.at[0, 1], core_sems.at[1, 1], sibling)

    def x_stage():
        pltpu.make_async_remote_copy(
            src_ref=core_in, dst_ref=core_in, send_sem=core_sems.at[0, 1], recv_sem=core_sems.at[1, 1],
            device_id=sibling, device_id_type=MESH,
        ).wait_recv()
        places = (
            (1 - xl) * 2 + xh, xl * 2 + (1 - xh), (1 - xl) * 2 + (1 - xh),
        )
        for index, q in enumerate(places):
            chip_out[index] = (part[2 * q + core] + core_in[q].astype(F32)).astype(BF16)
            sends.start(
                chip_out.at[index], chip_in.at[index], ip_sems.at[0, index], ip_sems.at[1, index], across[index]
            )

    for step in range(2, d.nz // 2 + 1):
        scatter_a_z.send(step)
        if step == 2:
            x_stage()
    for step in range(2, d.ny // 2 + 1):
        scatter_b_y.send(step)
    scatter_a_z.finish()
    scatter_a_y.send(1)
    scatter_b_y.finish()
    scatter_b_z.send(1)
    for step in range(2, d.ny // 2 + 1):
        scatter_a_y.send(step)
    for step in range(2, d.nz // 2 + 1):
        scatter_b_z.send(step)

    def restore(source, base, columns):
        for piece in range(columns // BLOCK):
            block = base // BLOCK + piece
            value = source[y, pl.ds(z_rows(z), rb), piece * BLOCK : (piece + 1) * BLOCK] * inverse_of(block)
            total = 0.0
            for _ in range(3):
                top = value.astype(BF16)
                total = total + jnp.dot(top, had[...], preferred_element_type=F32)
                value = value - top.astype(F32)
            source[y, pl.ds(z_rows(z), rb), piece * BLOCK : (piece + 1) * BLOCK] = total * (signs_of(block) * ROOT)
        near = pl.ds(pl.multiple_of(z_rows(z) + xl * d.rows, 8), d.rows)
        far = pl.ds(pl.multiple_of(z_rows(z) + (1 - xl) * d.rows, 8), d.rows)
        columns_at = pl.ds(pl.multiple_of(xl * hf + base, BLOCK), columns)
        which = 0 if base == 0 else 1
        sends.start(
            source.at[y, far, :], wg_ref.at[:, columns_at], fin_sems.at[0, which], fin_sems.at[1, which], partner
        )
        wg_ref[:, columns_at] = source[y, near, :]

    scatter_a_y.finish()
    restore(sa, 0, d.cols_a)
    scatter_b_z.finish()
    restore(sb, d.cols_a, d.cols_b)

    mine = xl * 2 + xh
    total = part[2 * mine + core] + core_in[mine].astype(F32)
    for index in range(3):
        slot = chip_in.at[index]
        pltpu.make_async_remote_copy(
            src_ref=slot, dst_ref=slot, send_sem=ip_sems.at[0, index], recv_sem=ip_sems.at[1, index],
            device_id=across[index], device_id_type=MESH,
        ).wait_recv()
        total = total + slot[...].astype(F32)
    ig_ref[...] = total.astype(BF16)

    landed(ug_ref.at[:, there], 4)
    for which, base, columns in ((0, 0, d.cols_a), (1, d.cols_a, d.cols_b)):
        slot = wg_ref.at[:, pl.ds(pl.multiple_of((1 - xl) * hf + base, BLOCK), columns)]
        pltpu.make_async_remote_copy(
            src_ref=slot, dst_ref=slot, send_sem=fin_sems.at[0, which], recv_sem=fin_sems.at[1, which],
            device_id=partner, device_id_type=MESH,
        ).wait_recv()
    sends.drain()


def local(ny, nz, layer_input, gate_weight, up_value, hidden_grad, sign_bits, scale_exponent):
    tokens, depth = layer_input.shape
    rows, hidden = gate_weight.shape
    d = Dims(ny, nz, tokens, depth, rows, hidden)
    t, hf, rb = d.tokens, d.half, d.rb
    hy, hz = ny // 2, nz // 2
    vm = lambda shape, dtype: pltpu.VMEM(shape, dtype)
    sem = lambda *shape: pltpu.SemaphoreType.DMA(shape)
    pair = lambda *shape: [sem(*shape), sem(*shape)]
    scratch = [
        vm((2, t, depth), BF16), vm((2, ny, d.yrows, 2 * t), BF16),
        vm((2, t, hf), BF16), vm((2, t, hf), BF16), vm((2, t, hf), BF16),
        vm((d.pad, hf), BF16), vm((d.pad, hf), BF16),
        vm((ny, d.yrows, d.cols_a), BF16), vm((ny, d.yrows, d.cols_b), BF16),
        vm((2 * t, d.cols_a), BF16), vm((2 * t, d.cols_b), BF16),
        vm((2, 2 * t, hf), BF16), vm((BLOCK, BLOCK), BF16),
        vm((ny, d.yrows, d.cols_a), F32), vm((ny, d.yrows, d.cols_b), F32),
        vm((ny, d.yrows, d.cols_a), BF16), vm((ny, d.yrows, d.cols_b), BF16),
        vm((2, hz, ny, rb, d.cols_a), BF16), vm((2, hy, rb, d.cols_a), BF16),
        vm((2, hy, d.yrows, d.cols_b), BF16), vm((2, hz, rb, d.cols_b), BF16),
        vm((8, t // 4, depth), F32), vm((4, t // 4, depth), BF16), vm((4, t // 4, depth), BF16),
        vm((3, t // 4, depth), BF16), vm((3, t // 4, depth), BF16),
        sem(2, 5), sem(2, 2), sem(2, 3), sem(2, 2), pltpu.SemaphoreType.DMA,
        *pair(2, hy, 2), *pair(2, hz, ny), *pair(2, hz, 2), *pair(2, hy, 4),
        *pair(2, hz, ny), *pair(2, hy, 2), *pair(2, hy, 4), *pair(2, hz, 2),
    ]
    whole = pl.BlockSpec(memory_space=pltpu.VMEM)
    return pl.pallas_call(
        functools.partial(kernel, d),
        out_shape=(
            jax.ShapeDtypeStruct((t // 4, depth), BF16),
            jax.ShapeDtypeStruct((t, hidden), BF16),
            jax.ShapeDtypeStruct((rows, hidden), F32),
        ),
        in_specs=[whole] * 5 + [pl.BlockSpec(memory_space=pltpu.SMEM)],
        out_specs=(whole,) * 3,
        scratch_shapes=scratch,
        compiler_params=pltpu.CompilerParams(
            collective_id=0, has_side_effects=True, vmem_limit_bytes=56 * 1024 * 1024
        ),
        name="gate_backward",
    )(layer_input, gate_weight, up_value, hidden_grad, sign_bits.reshape(1, hidden), scale_exponent)


def build(mesh, ny, nz):
    return jax.shard_map(
        functools.partial(local, ny, nz),
        mesh=mesh,
        in_specs=(P("dp", None), P("dp", "mp"), P("dp", "mp"), P("dp", "mp"), P("mp"), P("mp")),
        out_specs=(P(("dp", "mp"), None), P("dp", "mp"), P("dp", "mp")),
        check_vma=False,
    )


def solution(mesh):
    return build(mesh, 4, 8)
```

time: 817 us -> 128 us (0.16)
  waiting for transfers between devices: 718 us -> 0 us
  Pallas kernels: 0 us -> 122 us
  matrix products: 44.3 us -> 0 us
  other arithmetic: 16.4 us -> 0 us
  local copies, waits for them, and re-layouts: 20.6 us -> 5.46 us
  between operations: 13.8 us -> 0.64 us
    reduce_scatter x2 -> x0, waiting for transfers between devices: 418 us -> none  [the longest x1 418 us: local(): lax.psum_scatter(quantized.astype(jnp.float32), 'dp', scatter_dimension=0...]
    all_gather x1 -> x0, waiting for transfers between devices: 299 us -> none  [local(): full_weight = lax.all_gather(gate_weight, 'dp', axis=0, tiled=True)]
    pallas_call x0 -> x1, Pallas kernels: none -> 122 us  [local(): pl.pallas_call(functools.partial(kernel, d), out_shape=(jax.ShapeDtypeStr...]
    dot_general x5 -> x0, matrix products: 44.3 us -> none  [the longest x1 24.6 us: quantize(): jnp.einsum('rbk,kj->rbj', blocks, hadamard, precision=lax.Precision.HIGHEST)]
    convert_element_type x1 -> x0, local copies, waits for them, and re-layouts: 19.4 us -> none  [local(): quantized.astype(jnp.float32)]
    convert_element_type x4 -> x0, other arithmetic: 15.5 us -> none  [the longest x1 12.5 us: local(): quantized.astype(jnp.float32)]
  transfers between devices with their start and end apart: 3 -> 0, of which waited for: 2 -> 0; matrix products, arithmetic and copies ran while one was open for 8% -> 0% of each run, Pallas kernels for 0% -> 0%
where the time goes in v1:
time: 128 us
  Pallas kernels  122 us (95%)
  local copies, waits for them, and re-layouts  5.46 us (4%)
    pallas_call x1, Pallas kernels, local(): pl.pallas_call(functools.partial(kernel, d), out_shape=(jax.ShapeDtypeStr...  122 us
    unnamed x5, local copies, waits for them, and re-layouts  4.17 us

profile of v1, /device:TPU:8, one launch (start us, length us, event | category | flops | bytes accessed | tf_op | source)
XLA Modules:
  0.0 127.7 jit_solution(16114587491536463564)
XLA Ops:
  0.6 1.3 %reshape.9.bits_ref = s32[1,1792]{1,0:T(1,128)} reshape(s32[1792]{0:T(1024)} %param.10) | data formatting | bytes 14336 | tf_op jit(solution)/shard_map/reshape | solution.py:516
  1.9 121.6 %gate_backward.1 = (bf16[32,2560]{1,0:T(8,128)(2,1)}, bf16[128,1792]{1,0:T(8,128)(2,1)}, f32[40,1792]{1,0:T(8,128)}) custom-call(bf16[128,2560]{1,0:T(8,128)(2,1)} %x_ref.1, bf16[40,1792]{1,0:T(8,128)(2,1)} %w_ref.1, bf16[128,1792]{1,0:T(8,128)(2,1)} %up_ref.1, bf16[128,1792]{1,0:T(8,128)(2,1)} %hg_ref.1, s32[1,1792]{1,0:T(1,128)} %reshape.9.bits_ref, s32[14]{0:T(128)} %exp_ref.1), custom_call_target="tpu_custom_call" | custom-call | tf_op jit(solution)/shard_map/gate_backward/pallas_call | solution.py:502
  123.5 1.6 %copy.12 = bf16[32,2560]{1,0:T(8,128)(2,1)} copy(bf16[32,2560]{1,0:T(8,128)(2,1)} %get-tuple-element.6) | data formatting | bytes 327680
  125.1 0.0 copy-start
  125.1 1.9 %copy.13 = bf16[128,1792]{1,0:T(8,128)(2,1)} copy(bf16[128,1792]{1,0:T(8,128)(2,1)} %get-tuple-element.7) | data formatting | bytes 917504
  127.0 0.0 copy-done
  127.0 0.7 copy.14
Async XLA Ops:
  125.1 1.9 %copy-start = (f32[40,1792]{1,0:T(8,128)S(1)}, f32[40,1792]{1,0:T(8,128)}, u32[]{:S(2)}) copy-start(f32[40,1792]{1,0:T(8,128)} %get-tuple-element.8) | copy-start | bytes 860164

commit v2 on v1

--- a/solution.py
+++ b/solution.py
@@ -32,8 +32,6 @@
         self.pad = up_to(rows, 16)
         cut = up_to(self.rb // 2, 16)
         self.row_subs = ((0, cut), (cut, self.rb - cut))
-        quarter = self.yrows // 4
-        self.y_subs = tuple((s * quarter, quarter) for s in range(4))
 
 
 class Ring:
@@ -64,7 +62,12 @@
 
 
 def went(side, sub, count):
-    return (sub < (count + 1) // 2) == (side == 0)
+    return sub % 2 == side
+
+
+def nearest_first(length):
+    half = length // 2
+    return [0] + [sign * hops for hops in range(1, half) for sign in (1, -1)] + [half]
 
 
 class Gather:
@@ -83,9 +86,9 @@
             device_id=self.ring.sides[side], device_id_type=MESH,
         ).wait_recv()
 
-    def send(self, step):
+    def send(self, step, subs=None):
         last = step == self.ring.half
-        for sub in range(self.count):
+        for sub in range(self.count) if subs is None else subs:
             for side in (0, 1):
                 if step > 1:
                     self.wait_one(side, step - 1, sub)
@@ -126,9 +129,9 @@
         ).wait_recv()
         return here[...].astype(F32)
 
-    def send(self, step):
+    def send(self, step, subs=None):
         far = self.ring.half + 1 - step
-        for sub in range(self.count):
+        for sub in range(self.count) if subs is None else subs:
             for side in (0, 1):
                 if step == 1 and not went(side, sub, self.count):
                     continue
@@ -145,8 +148,8 @@
                     self.ring.sides[side],
                 )
 
-    def finish(self):
-        for sub in range(self.count):
+    def finish(self, subs=None):
+        for sub in range(self.count) if subs is None else subs:
             mine = self.own(self.ring.me, sub)
             total = mine[...]
             for side in (0, 1):
@@ -169,10 +172,10 @@
     dims,
     x_ref, w_ref, up_ref, hg_ref, bits_ref, exp_ref,
     ig_ref, ug_ref, wg_ref,
-    x2, xt, hg2, up2, upg2, wsend, wrecv, wa, wb, g_a, g_b, turned, had,
+    w_own, bits, x2, xt, hg2, up2, upg2, wsend, wrecv, wa, wb, g_a, g_b, turned, had,
     sa, sb, oa, ob, la_z, la_y, lb_y, lb_z,
     part, core_out, core_in, chip_out, chip_in,
-    x_sems, core_sems, ip_sems, fin_sems, local_sem,
+    x_sems, core_sems, ip_sems, fin_sems, local_sems,
     ga_y_s, ga_y_r, ga_z_s, ga_z_r, gb_z_s, gb_z_r, gb_y_s, gb_y_r,
     ra_z_s, ra_z_r, ra_y_s, ra_y_r, rb_y_s, rb_y_r, rb_z_s, rb_z_r,
 ):
@@ -197,15 +200,31 @@
         pl.semaphore_signal(barrier, inc=1, device_id=other, device_id_type=MESH)
 
     sends = Sends()
+    loads = []
+
+    def load(src, dst):
+        copy = pltpu.make_async_copy(src, dst, local_sems.at[len(loads)])
+        copy.start()
+        loads.append(copy)
+
     here = pl.ds(pl.multiple_of(xl * hf, BLOCK), hf)
     there = pl.ds(pl.multiple_of((1 - xl) * hf, BLOCK), hf)
 
+    load(w_ref, w_own)
+    load(x_ref, x2.at[xl])
+    load(hg_ref.at[:, here], hg2.at[xl])
+    load(up_ref.at[:, here], up2.at[xl])
+    for block in range(d.blocks):
+        at = pl.ds(pl.multiple_of(xl * hf + block * BLOCK, BLOCK), BLOCK)
+        load(bits_ref.at[at], bits.at[block])
+
     def padded(columns):
-        rows = w_ref[:, columns].astype(F32)
+        rows = w_own[:, columns].astype(F32)
         if d.pad == d.rows:
             return rows
         return jnp.concatenate([rows, jnp.zeros((d.pad - d.rows, hf), F32)], axis=0)
 
+    loads[0].wait()
     wsend[...] = padded(there).astype(BF16)
     pl.semaphore_wait(barrier, len(others))
 
@@ -214,8 +233,6 @@
     sends.start(x_ref.at[x_rows, :], x2.at[xl, x_rows, :], x_sems.at[0, 1], x_sems.at[1, 1], partner)
     sends.start(hg_ref.at[:, there], hg2.at[xl], x_sems.at[0, 2], x_sems.at[1, 2], partner)
     sends.start(up_ref.at[:, there], up2.at[xl], x_sems.at[0, 3], x_sems.at[1, 3], partner)
-    own_x = pltpu.make_async_copy(x_ref, x2.at[xl], local_sem)
-    own_x.start()
 
     def landed(ref, index):
         pltpu.make_async_remote_copy(
@@ -224,18 +241,29 @@
         ).wait_recv()
 
     z_rows = lambda place: pl.multiple_of(place * rb, 16)
-    ra = lambda ref: lambda place, sub: ref.at[place, pl.ds(z_rows(z) + d.row_subs[sub][0], d.row_subs[sub][1]), :]
-    rz = lambda ref: lambda place, sub: ref.at[sub, pl.ds(z_rows(place), rb), :]
-    rbz = lambda ref: lambda place, sub: ref.at[y, pl.ds(z_rows(place) + d.row_subs[sub][0], d.row_subs[sub][1]), :]
-    rby = lambda ref: lambda place, sub: ref.at[place, pl.ds(d.y_subs[sub][0], d.y_subs[sub][1]), :]
-
-    gather_a_y = Gather(ring_y, 2, ra(wa), (ga_y_s, ga_y_r), sends)
-    gather_a_z = Gather(ring_z, d.ny, rz(wa), (ga_z_s, ga_z_r), sends)
-    gather_b_z = Gather(ring_z, 2, rbz(wb), (gb_z_s, gb_z_r), sends)
-    gather_b_y = Gather(ring_y, 4, rby(wb), (gb_y_s, gb_y_r), sends)
+    near_y, near_z = nearest_first(d.ny), nearest_first(d.nz)
+    far_y, far_z = near_y[::-1], near_z[::-1]
+    part_of = lambda place, sub: pl.ds(z_rows(place) + d.row_subs[sub][0], d.row_subs[sub][1])
+
+    def along_y(ref):
+        return lambda place, sub: ref.at[place, part_of(z, sub), :]
+
+    def along_z(ref):
+        return lambda place, sub: ref.at[y, part_of(place, sub), :]
+
+    def along_z_of_y(ref, offsets):
+        return lambda place, sub: ref.at[ring_y.place(offsets[sub]), pl.ds(z_rows(place), rb), :]
+
+    def along_y_of_z(ref, offsets):
+        return lambda place, sub: ref.at[place, pl.ds(z_rows(ring_z.place(offsets[sub])), rb), :]
+
+    gather_a_y = Gather(ring_y, 2, along_y(wa), (ga_y_s, ga_y_r), sends)
+    gather_a_z = Gather(ring_z, d.ny, along_z_of_y(wa, near_y), (ga_z_s, ga_z_r), sends)
+    gather_b_z = Gather(ring_z, 2, along_z(wb), (gb_z_s, gb_z_r), sends)
+    gather_b_y = Gather(ring_y, d.nz, along_y_of_z(wb, near_z), (gb_y_s, gb_y_r), sends)
 
     landed(wrecv, 0)
-    own_rows = w_ref[:, here].astype(F32)
+    own_rows = w_own[:, here].astype(F32)
     other_rows = wrecv[...].astype(F32)[: d.rows]
     low = jnp.where(xl == 0, own_rows, other_rows)
     high = jnp.where(xl == 0, other_rows, own_rows)
@@ -243,52 +271,67 @@
     wa[y, pl.ds(z_rows(z), rb), :] = rows[:, : d.cols_a]
     wb[y, pl.ds(z_rows(z), rb), :] = rows[:, d.cols_a :]
 
+    per_y = d.yrows // BLOCK
+
+    def turn(replica, place):
+        @pl.loop(0, per_y)
+        def _(chunk):
+            at = pl.ds(pl.multiple_of(chunk * BLOCK, BLOCK), BLOCK)
+            tile = x2[replica, :, pl.ds(pl.multiple_of(place * d.yrows + chunk * BLOCK, BLOCK), BLOCK)]
+            tile = tile.astype(F32).T.astype(BF16)
+            xt[replica, place, at, 0:t] = tile
+            xt[replica, place, at, t : 2 * t] = tile
+
+    gather_b_z.send(1)
     gather_a_y.send(1)
-    gather_b_z.send(1)
+    gather_b_y.send(1, [0])
+    gather_a_z.send(1, [0])
     had[...] = hadamard_signs()
-    for step in range(2, d.ny // 2 + 1):
-        gather_a_y.send(step)
+    gather_b_z.send(2)
+    gather_b_y.send(1, [1, 2])
+    gather_a_y.send(2)
+    gather_a_z.send(1, [1, 2])
+    loads[1].wait()
+    turn(xl, 0)
+    gather_b_z.send(3)
+    gather_b_y.send(1, [3, 4])
     gather_a_y.finish()
-    gather_a_z.send(1)
-    for step in range(2, d.nz // 2 + 1):
-        gather_b_z.send(step)
+    gather_a_z.send(1, [3])
+    gather_a_z.send(2, [0])
+    turn(xl, 1)
+    gather_b_z.send(4)
+    gather_b_y.send(1, [5, 6])
+    gather_a_z.send(2, [1, 2])
+    turn(xl, 2)
     gather_b_z.finish()
-    gather_b_y.send(1)
-
-    own_x.wait()
+    gather_b_y.send(1, [7])
+    gather_b_y.send(2, [0, 1, 2])
+    gather_a_z.send(2, [3])
+    turn(xl, 3)
+    gather_a_z.send(3, [0, 1])
     theirs = x2.at[1 - xl, x_rows, :]
     landed(theirs, 1)
     sends.start(theirs, theirs, core_sems.at[0, 0], core_sems.at[1, 0], sibling)
-
-    per_y = d.yrows // BLOCK
-
-    def turn(replica):
-        @pl.loop(0, d.depth // BLOCK)
-        def _(chunk):
-            tile = x2[replica, :, pl.ds(pl.multiple_of(chunk * BLOCK, BLOCK), BLOCK)]
-            tile = tile.astype(F32).T.astype(BF16)
-            at = pl.ds(pl.multiple_of(lax.rem(chunk, per_y) * BLOCK, BLOCK), BLOCK)
-            xt[replica, lax.div(chunk, per_y), at, 0:t] = tile
-            xt[replica, lax.div(chunk, per_y), at, t : 2 * t] = tile
-
-    turn(xl)
-    for step in range(2, d.nz // 2 + 1):
-        gather_a_z.send(step)
-        if step == 2:
-            other_x = pl.ds(pl.multiple_of((1 - core) * (t // 2), 16), t // 2)
-            rest = x2.at[1 - xl, other_x, :]
-            pltpu.make_async_remote_copy(
-                src_ref=rest, dst_ref=rest, send_sem=core_sems.at[0, 0], recv_sem=core_sems.at[1, 0],
-                device_id=sibling, device_id_type=MESH,
-            ).wait_recv()
-    turn(1 - xl)
-    for step in range(2, d.ny // 2 + 1):
-        gather_b_y.send(step)
+    gather_a_z.send(3, [2, 3])
+    gather_b_y.send(2, [3, 4])
+    other_x = pl.ds(pl.multiple_of((1 - core) * (t // 2), 16), t // 2)
+    rest = x2.at[1 - xl, other_x, :]
+    pltpu.make_async_remote_copy(
+        src_ref=rest, dst_ref=rest, send_sem=core_sems.at[0, 0], recv_sem=core_sems.at[1, 0],
+        device_id=sibling, device_id_type=MESH,
+    ).wait_recv()
+    turn(1 - xl, 0)
+    gather_a_z.send(4, [0, 1])
+    turn(1 - xl, 1)
+    gather_b_y.send(2, [5, 6])
+    gather_a_z.send(4, [2, 3])
+    turn(1 - xl, 2)
+    gather_b_y.send(2, [7])
+    turn(1 - xl, 3)
     landed(hg2.at[1 - xl], 2)
     landed(up2.at[1 - xl], 3)
-    hg2[xl] = hg_ref[:, here]
-    up2[xl] = up_ref[:, here]
-    gather_a_z.finish()
+    for copy in loads[2:]:
+        copy.wait()
     gather_b_y.finish()
 
     def scale_of(block):
@@ -298,8 +341,7 @@
         return jnp.right_shift(64, exp_ref[xl * d.blocks + block]).astype(F32) * (1.0 / 64.0)
 
     def signs_of(block):
-        bits = bits_ref[:, pl.ds(pl.multiple_of(xl * hf + block * BLOCK, BLOCK), BLOCK)]
-        return (1 - 2 * bits).astype(F32)
+        return (1 - 2 * bits[block : block + 1, :]).astype(F32)
 
     def gate_tile(w_part, g_part, base, start, width):
         columns = slice(start, start + width)
@@ -330,14 +372,6 @@
                 turned[replica, 0:t, put] = top[mine]
                 turned[replica, t : 2 * t, put] = rest[mine]
 
-    for start in range(0, d.cols_b, 2 * BLOCK):
-        gate_tile(wb, g_b, d.cols_a, start, min(2 * BLOCK, d.cols_b - start))
-    for start in range(0, d.cols_a, 2 * BLOCK):
-        gate_tile(wa, g_a, 0, start, min(2 * BLOCK, d.cols_a - start))
-
-    sends.start(upg2.at[1 - xl], ug_ref.at[:, here], x_sems.at[0, 4], x_sems.at[1, 4], partner)
-    ug_ref[:, here] = upg2[xl]
-
     def quantized(lhs, replica, columns):
         value = jnp.dot(lhs, turned[replica, :, columns], preferred_element_type=F32)
         return jnp.clip(value, -127.0, 127.0).astype(BF16).astype(F32)
@@ -367,18 +401,30 @@
 
     at_sub = lambda ref: lambda side, step, sub: ref.at[side, step, sub]
     at_rows = lambda ref: lambda side, step, sub: ref.at[side, step, pl.ds(d.row_subs[sub][0], d.row_subs[sub][1]), :]
-    at_y = lambda ref: lambda side, step, sub: ref.at[side, step, pl.ds(d.y_subs[sub][0], d.y_subs[sub][1]), :]
-    scatter_a_z = Scatter(ring_z, d.ny, rz(sa), rz(oa), at_sub(la_z), (ra_z_s, ra_z_r), sends)
-    scatter_a_y = Scatter(ring_y, 2, ra(sa), ra(oa), at_rows(la_y), (ra_y_s, ra_y_r), sends)
-    scatter_b_y = Scatter(ring_y, 4, rby(sb), rby(ob), at_y(lb_y), (rb_y_s, rb_y_r), sends)
-    scatter_b_z = Scatter(ring_z, 2, rbz(sb), rbz(ob), at_rows(lb_z), (rb_z_s, rb_z_r), sends)
-
+    scatter_a_z = Scatter(
+        ring_z, d.ny, along_z_of_y(sa, far_y), along_z_of_y(oa, far_y), at_sub(la_z), (ra_z_s, ra_z_r), sends
+    )
+    scatter_a_y = Scatter(ring_y, 2, along_y(sa), along_y(oa), at_rows(la_y), (ra_y_s, ra_y_r), sends)
+    scatter_b_y = Scatter(
+        ring_y, d.nz, along_y_of_z(sb, far_z), along_y_of_z(ob, far_z), at_sub(lb_y), (rb_y_s, rb_y_r), sends
+    )
+    scatter_b_z = Scatter(ring_z, 2, along_z(sb), along_z(ob), at_rows(lb_z), (rb_z_s, rb_z_r), sends)
+
+    for start in range(0, d.cols_b, 2 * BLOCK):
+        gate_tile(wb, g_b, d.cols_a, start, min(2 * BLOCK, d.cols_b - start))
     grads_b(0, 1)
     scatter_b_y.send(1)
+    gather_a_z.finish()
+    for start in range(0, d.cols_a, 2 * BLOCK):
+        gate_tile(wa, g_a, 0, start, min(2 * BLOCK, d.cols_a - start))
     grads_a(0, 1)
     scatter_a_z.send(1)
-    grads_a(1, d.nz)
-    grads_b(1, d.ny)
+    sends.start(upg2.at[1 - xl], ug_ref.at[:, here], x_sems.at[0, 4], x_sems.at[1, 4], partner)
+    ug_ref[:, here] = upg2[xl]
+    grads_a(1, 3)
+    grads_b(1, 3)
+    scatter_a_z.send(2)
+    scatter_b_y.send(2, [0, 1, 2])
 
     def partial_tile(place):
         total = 0.0
@@ -412,20 +458,29 @@
                 chip_out.at[index], chip_in.at[index], ip_sems.at[0, index], ip_sems.at[1, index], across[index]
             )
 
-    for step in range(2, d.nz // 2 + 1):
-        scatter_a_z.send(step)
-        if step == 2:
-            x_stage()
-    for step in range(2, d.ny // 2 + 1):
-        scatter_b_y.send(step)
-    scatter_a_z.finish()
+    grads_a(3, 5)
+    scatter_a_z.send(3)
+    scatter_b_y.send(2, [3, 4])
+    x_stage()
+    grads_b(3, 4)
+    scatter_b_y.send(2, [5, 6, 7])
+    grads_a(5, 8)
+    scatter_b_y.finish([0])
+    scatter_b_z.send(1)
+    scatter_a_z.send(4, [0, 1])
+    scatter_b_y.finish([1, 2])
+    scatter_b_z.send(2)
+    scatter_a_z.send(4, [2, 3])
+    scatter_b_y.finish([3, 4])
+    scatter_b_z.send(3)
+    scatter_a_z.finish([0])
     scatter_a_y.send(1)
-    scatter_b_y.finish()
-    scatter_b_z.send(1)
-    for step in range(2, d.ny // 2 + 1):
-        scatter_a_y.send(step)
-    for step in range(2, d.nz // 2 + 1):
-        scatter_b_z.send(step)
+    scatter_b_y.finish([5, 6])
+    scatter_b_z.send(4)
+    scatter_a_z.finish([1, 2])
+    scatter_a_y.send(2)
+    scatter_b_y.finish([7])
+    scatter_a_z.finish([3])
 
     def restore(source, base, columns):
         for piece in range(columns // BLOCK):
@@ -472,6 +527,12 @@
     sends.drain()
 
 
+def hand_over(a_ref, b_ref, c_ref, a_out, b_out, c_out):
+    a_out[...] = a_ref[...]
+    b_out[...] = b_ref[...]
+    c_out[...] = c_ref[...]
+
+
 def local(ny, nz, layer_input, gate_weight, up_value, hidden_grad, sign_bits, scale_exponent):
     tokens, depth = layer_input.shape
     rows, hidden = gate_weight.shape
@@ -482,6 +543,7 @@
     sem = lambda *shape: pltpu.SemaphoreType.DMA(shape)
     pair = lambda *shape: [sem(*shape), sem(*shape)]
     scratch = [
+        vm((rows, hidden), BF16), vm((8, BLOCK), jnp.int32),
         vm((2, t, depth), BF16), vm((2, ny, d.yrows, 2 * t), BF16),
         vm((2, t, hf), BF16), vm((2, t, hf), BF16), vm((2, t, hf), BF16),
         vm((d.pad, hf), BF16), vm((d.pad, hf), BF16),
@@ -491,29 +553,37 @@
         vm((ny, d.yrows, d.cols_a), F32), vm((ny, d.yrows, d.cols_b), F32),
         vm((ny, d.yrows, d.cols_a), BF16), vm((ny, d.yrows, d.cols_b), BF16),
         vm((2, hz, ny, rb, d.cols_a), BF16), vm((2, hy, rb, d.cols_a), BF16),
-        vm((2, hy, d.yrows, d.cols_b), BF16), vm((2, hz, rb, d.cols_b), BF16),
+        vm((2, hy, nz, rb, d.cols_b), BF16), vm((2, hz, rb, d.cols_b), BF16),
         vm((8, t // 4, depth), F32), vm((4, t // 4, depth), BF16), vm((4, t // 4, depth), BF16),
         vm((3, t // 4, depth), BF16), vm((3, t // 4, depth), BF16),
-        sem(2, 5), sem(2, 2), sem(2, 3), sem(2, 2), pltpu.SemaphoreType.DMA,
-        *pair(2, hy, 2), *pair(2, hz, ny), *pair(2, hz, 2), *pair(2, hy, 4),
-        *pair(2, hz, ny), *pair(2, hy, 2), *pair(2, hy, 4), *pair(2, hz, 2),
+        sem(2, 5), sem(2, 2), sem(2, 3), sem(2, 2), sem(4 + d.blocks),
+        *pair(2, hy, 2), *pair(2, hz, ny), *pair(2, hz, 2), *pair(2, hy, nz),
+        *pair(2, hz, ny), *pair(2, hy, 2), *pair(2, hy, nz), *pair(2, hz, 2),
     ]
     whole = pl.BlockSpec(memory_space=pltpu.VMEM)
-    return pl.pallas_call(
+    anywhere = pl.BlockSpec(memory_space=pl.ANY)
+    results = pl.pallas_call(
         functools.partial(kernel, d),
         out_shape=(
             jax.ShapeDtypeStruct((t // 4, depth), BF16),
             jax.ShapeDtypeStruct((t, hidden), BF16),
             jax.ShapeDtypeStruct((rows, hidden), F32),
         ),
-        in_specs=[whole] * 5 + [pl.BlockSpec(memory_space=pltpu.SMEM)],
+        in_specs=[anywhere] * 5 + [pl.BlockSpec(memory_space=pltpu.SMEM)],
         out_specs=(whole,) * 3,
         scratch_shapes=scratch,
         compiler_params=pltpu.CompilerParams(
             collective_id=0, has_side_effects=True, vmem_limit_bytes=56 * 1024 * 1024
         ),
         name="gate_backward",
-    )(layer_input, gate_weight, up_value, hidden_grad, sign_bits.reshape(1, hidden), scale_exponent)
+    )(layer_input, gate_weight, up_value, hidden_grad, sign_bits, scale_exponent)
+    return pl.pallas_call(
+        hand_over,
+        out_shape=tuple(jax.ShapeDtypeStruct(r.shape, r.dtype) for r in results),
+        in_specs=[whole] * 3,
+        out_specs=(whole,) * 3,
+        name="hand_over",
+    )(*results)
 
 
 def build(mesh, ny, nz):

time: 128 us -> 90.2 us (0.70)
  Pallas kernels: 122 us -> 89.5 us
  local copies, waits for them, and re-layouts: 5.46 us -> 0 us
    pallas_call x1, Pallas kernels: 122 us -> 87.3 us  [local(): pl.pallas_call(functools.partial(kernel, d), out_shape=(jax.ShapeDtypeStr...]
    unnamed x5 -> x0, local copies, waits for them, and re-layouts: 4.17 us -> none
    pallas_call x0 -> x1, Pallas kernels: none -> 2.12 us  [local(): pl.pallas_call(hand_over, out_shape=tuple((jax.ShapeDtypeStruct(r.shape,...]
    reshape x1 -> x0, local copies, waits for them, and re-layouts: 1.3 us -> none  [local(): sign_bits.reshape(1, hidden)]
where the time goes in v2:
time: 90.2 us; the launch traced here: 90.1 us
  Pallas kernels  89.5 us (99%)
    pallas_call x1, Pallas kernels, local(): pl.pallas_call(functools.partial(kernel, d), out_shape=(jax.ShapeDtypeStr...  87.3 us
    pallas_call x1, Pallas kernels, local(): pl.pallas_call(hand_over, out_shape=tuple((jax.ShapeDtypeStruct(r.shape,...  2.12 us

profile of v2, /device:TPU:8, one launch (start us, length us, event | category | flops | bytes accessed | tf_op | source)
XLA Modules:
  0.0 90.1 jit_solution(3210215184915399775)
XLA Ops:
  0.6 87.3 %gate_backward.1 = (bf16[32,2560]{1,0:T(8,128)(2,1)}, bf16[128,1792]{1,0:T(8,128)(2,1)}, f32[40,1792]{1,0:T(8,128)}) custom-call(bf16[128,2560]{1,0:T(8,128)(2,1)} %x_ref.1, bf16[40,1792]{1,0:T(8,128)(2,1)} %w_ref.1, bf16[128,1792]{1,0:T(8,128)(2,1)} %up_ref.1, bf16[128,1792]{1,0:T(8,128)(2,1)} %hg_ref.1, s32[1792]{0:T(1024)} %bits_ref.1, s32[14]{0:T(128)} %exp_ref.1), custom_call_target="tpu_custom_call" | custom-call | tf_op jit(solution)/shard_map/gate_backward/pallas_call | solution.py:565
  88.0 2.1 %hand_over.1 = (bf16[32,2560]{1,0:T(8,128)(2,1)}, bf16[128,1792]{1,0:T(8,128)(2,1)}, f32[40,1792]{1,0:T(8,128)}) custom-call(bf16[32,2560]{1,0:T(8,128)(2,1)} %get-tuple-element.6.a_ref, bf16[128,1792]{1,0:T(8,128)(2,1)} %get-tuple-element.7.b_ref, f32[40,1792]{1,0:T(8,128)} %get-tuple-element.8.c_ref), custom_call_target="tpu_custom_call" | custom-call | tf_op jit(solution)/shard_map/hand_over/pallas_call | solution.py:580

commit v3 on v2

--- a/solution.py
+++ b/solution.py
@@ -172,7 +172,7 @@
     dims,
     x_ref, w_ref, up_ref, hg_ref, bits_ref, exp_ref,
     ig_ref, ug_ref, wg_ref,
-    w_own, bits, x2, xt, hg2, up2, upg2, wsend, wrecv, wa, wb, g_a, g_b, turned, had,
+    w_own, bits, x2, xt, hg2, up2, upg2, wsend, wrecv, early_b, wa, wb, g_a, g_b, turned, had,
     sa, sb, oa, ob, la_z, la_y, lb_y, lb_z,
     part, core_out, core_in, chip_out, chip_in,
     x_sems, core_sems, ip_sems, fin_sems, local_sems,
@@ -195,7 +195,8 @@
     across = (partner, device(xh=1 - xh), device(xl=1 - xl, xh=1 - xh))
 
     barrier = pltpu.get_barrier_semaphore()
-    others = ring_y.sides + ring_z.sides + across + (sibling,)
+    opposite = device(y=ring_y.place(2))
+    others = ring_y.sides + (opposite,) + ring_z.sides + across + (sibling,)
     for other in others:
         pl.semaphore_signal(barrier, inc=1, device_id=other, device_id_type=MESH)
 
@@ -228,7 +229,10 @@
     wsend[...] = padded(there).astype(BF16)
     pl.semaphore_wait(barrier, len(others))
 
-    sends.start(wsend, wrecv, x_sems.at[0, 0], x_sems.at[1, 0], partner)
+    for index, columns in ((0, slice(d.cols_a, hf)), (5, slice(0, d.cols_a))):
+        sends.start(
+            wsend.at[:, columns], wrecv.at[:, columns], x_sems.at[0, index], x_sems.at[1, index], partner
+        )
     x_rows = pl.ds(pl.multiple_of(core * (t // 2), 16), t // 2)
     sends.start(x_ref.at[x_rows, :], x2.at[xl, x_rows, :], x_sems.at[0, 1], x_sems.at[1, 1], partner)
     sends.start(hg_ref.at[:, there], hg2.at[xl], x_sems.at[0, 2], x_sems.at[1, 2], partner)
@@ -245,9 +249,6 @@
     far_y, far_z = near_y[::-1], near_z[::-1]
     part_of = lambda place, sub: pl.ds(z_rows(place) + d.row_subs[sub][0], d.row_subs[sub][1])
 
-    def along_y(ref):
-        return lambda place, sub: ref.at[place, part_of(z, sub), :]
-
     def along_z(ref):
         return lambda place, sub: ref.at[y, part_of(place, sub), :]
 
@@ -257,19 +258,18 @@
     def along_y_of_z(ref, offsets):
         return lambda place, sub: ref.at[place, pl.ds(z_rows(ring_z.place(offsets[sub])), rb), :]
 
-    gather_a_y = Gather(ring_y, 2, along_y(wa), (ga_y_s, ga_y_r), sends)
     gather_a_z = Gather(ring_z, d.ny, along_z_of_y(wa, near_y), (ga_z_s, ga_z_r), sends)
     gather_b_z = Gather(ring_z, 2, along_z(wb), (gb_z_s, gb_z_r), sends)
     gather_b_y = Gather(ring_y, d.nz, along_y_of_z(wb, near_z), (gb_y_s, gb_y_r), sends)
 
-    landed(wrecv, 0)
-    own_rows = w_own[:, here].astype(F32)
-    other_rows = wrecv[...].astype(F32)[: d.rows]
-    low = jnp.where(xl == 0, own_rows, other_rows)
-    high = jnp.where(xl == 0, other_rows, own_rows)
-    rows = jnp.concatenate([low, high], axis=0).astype(BF16)
-    wa[y, pl.ds(z_rows(z), rb), :] = rows[:, : d.cols_a]
-    wb[y, pl.ds(z_rows(z), rb), :] = rows[:, d.cols_a :]
+    def assemble(index, columns, width, target):
+        landed(wrecv.at[:, columns], index)
+        own_at = pl.ds(pl.multiple_of(xl * hf + columns.start, BLOCK), width)
+        own_rows = w_own[:, own_at].astype(F32)
+        other_rows = wrecv[:, columns].astype(F32)[: d.rows]
+        low = jnp.where(xl == 0, own_rows, other_rows)
+        high = jnp.where(xl == 0, other_rows, own_rows)
+        target[y, pl.ds(z_rows(z), rb), :] = jnp.concatenate([low, high], axis=0).astype(BF16)
 
     per_y = d.yrows // BLOCK
 
@@ -282,20 +282,39 @@
             xt[replica, place, at, 0:t] = tile
             xt[replica, place, at, t : 2 * t] = tile
 
+    hops_y = (1, -1, 2)
+
+    def block_a(place):
+        return wa.at[place, pl.ds(z_rows(z), rb), :]
+
+    def come_a(index):
+        ref = block_a(ring_y.place(-hops_y[index]))
+        pltpu.make_async_remote_copy(
+            src_ref=ref, dst_ref=ref, send_sem=ga_y_s.at[index], recv_sem=ga_y_r.at[index],
+            device_id=opposite, device_id_type=MESH,
+        ).wait_recv()
+
+    assemble(0, slice(d.cols_a, hf), d.cols_b, wb)
     gather_b_z.send(1)
-    gather_a_y.send(1)
     gather_b_y.send(1, [0])
+    assemble(5, slice(0, d.cols_a), d.cols_a, wa)
+    for index in (2, 0, 1):
+        sends.start(
+            block_a(y), block_a(y), ga_y_s.at[index], ga_y_r.at[index],
+            device(y=ring_y.place(hops_y[index])),
+        )
     gather_a_z.send(1, [0])
     had[...] = hadamard_signs()
     gather_b_z.send(2)
     gather_b_y.send(1, [1, 2])
-    gather_a_y.send(2)
+    come_a(0)
+    come_a(1)
     gather_a_z.send(1, [1, 2])
     loads[1].wait()
     turn(xl, 0)
     gather_b_z.send(3)
     gather_b_y.send(1, [3, 4])
-    gather_a_y.finish()
+    come_a(2)
     gather_a_z.send(1, [3])
     gather_a_z.send(2, [0])
     turn(xl, 1)
@@ -332,26 +351,35 @@
     landed(up2.at[1 - xl], 3)
     for copy in loads[2:]:
         copy.wait()
-    gather_b_y.finish()
-
-    def scale_of(block):
-        return jnp.left_shift(1, exp_ref[xl * d.blocks + block]).astype(F32)
-
-    def inverse_of(block):
-        return jnp.right_shift(64, exp_ref[xl * d.blocks + block]).astype(F32) * (1.0 / 64.0)
-
-    def signs_of(block):
-        return (1 - 2 * bits[block : block + 1, :]).astype(F32)
-
-    def gate_tile(w_part, g_part, base, start, width):
-        columns = slice(start, start + width)
-        gate = jnp.zeros((2 * t, width), F32)
-        for place in range(d.ny):
-            at = slice(place * d.yrows, (place + 1) * d.yrows)
-            gate = gate + jnp.dot(
+
+    def gate_sum(w_part, columns, places):
+        total = 0.0
+        for place in places:
+            at = pl.ds(pl.multiple_of(place * d.yrows, BLOCK), d.yrows)
+            total = total + jnp.dot(
                 x2[:, :, at].reshape(2 * t, d.yrows), w_part[place, :, columns],
                 preferred_element_type=F32,
             )
+        return total
+
+    tiles_b = [(start, min(2 * BLOCK, d.cols_b - start)) for start in range(0, d.cols_b, 2 * BLOCK)]
+    tiles_a = [(start, min(2 * BLOCK, d.cols_a - start)) for start in range(0, d.cols_a, 2 * BLOCK)]
+    early = [ring_y.place(hops) for hops in (0, 1, -1)]
+    for start, width in tiles_b:
+        early_b[:, start : start + width] = gate_sum(wb, slice(start, start + width), early)
+    gather_b_y.finish()
+
+    def scale_of(block):
+        return jnp.left_shift(1, exp_ref[xl * d.blocks + block]).astype(F32)
+
+    def inverse_of(block):
+        return jnp.right_shift(64, exp_ref[xl * d.blocks + block]).astype(F32) * (1.0 / 64.0)
+
+    def signs_of(block):
+        return (1 - 2 * bits[block : block + 1, :]).astype(F32)
+
+    def gate_tile(gate, g_part, base, start, width):
+        columns = slice(start, start + width)
         at = slice(base + start, base + start + width)
         grad = hg2[:, :, at].reshape(2 * t, width).astype(F32)
         up = up2[:, :, at].reshape(2 * t, width).astype(F32)
@@ -404,19 +432,20 @@
     scatter_a_z = Scatter(
         ring_z, d.ny, along_z_of_y(sa, far_y), along_z_of_y(oa, far_y), at_sub(la_z), (ra_z_s, ra_z_r), sends
     )
-    scatter_a_y = Scatter(ring_y, 2, along_y(sa), along_y(oa), at_rows(la_y), (ra_y_s, ra_y_r), sends)
     scatter_b_y = Scatter(
         ring_y, d.nz, along_y_of_z(sb, far_z), along_y_of_z(ob, far_z), at_sub(lb_y), (rb_y_s, rb_y_r), sends
     )
     scatter_b_z = Scatter(ring_z, 2, along_z(sb), along_z(ob), at_rows(lb_z), (rb_z_s, rb_z_r), sends)
 
-    for start in range(0, d.cols_b, 2 * BLOCK):
-        gate_tile(wb, g_b, d.cols_a, start, min(2 * BLOCK, d.cols_b - start))
+    for start, width in tiles_b:
+        columns = slice(start, start + width)
+        gate = early_b[:, columns] + gate_sum(wb, columns, [ring_y.place(2)])
+        gate_tile(gate, g_b, d.cols_a, start, width)
     grads_b(0, 1)
     scatter_b_y.send(1)
     gather_a_z.finish()
-    for start in range(0, d.cols_a, 2 * BLOCK):
-        gate_tile(wa, g_a, 0, start, min(2 * BLOCK, d.cols_a - start))
+    for start, width in tiles_a:
+        gate_tile(gate_sum(wa, slice(start, start + width), range(d.ny)), g_a, 0, start, width)
     grads_a(0, 1)
     scatter_a_z.send(1)
     sends.start(upg2.at[1 - xl], ug_ref.at[:, here], x_sems.at[0, 4], x_sems.at[1, 4], partner)
@@ -473,12 +502,21 @@
     scatter_a_z.send(4, [2, 3])
     scatter_b_y.finish([3, 4])
     scatter_b_z.send(3)
-    scatter_a_z.finish([0])
-    scatter_a_y.send(1)
+    def pass_a(sub):
+        scatter_a_z.finish([sub])
+        index = hops_y.index({0: 2, 1: -1, 2: 1}[sub])
+        target = ring_y.place(hops_y[index])
+        at = pl.ds(z_rows(z), rb)
+        oa[target, at, :] = sa[target, at, :].astype(BF16)
+        sends.start(
+            oa.at[target, at, :], la_y.at[index], ra_y_s.at[index], ra_y_r.at[index], device(y=target)
+        )
+
+    pass_a(0)
     scatter_b_y.finish([5, 6])
     scatter_b_z.send(4)
-    scatter_a_z.finish([1, 2])
-    scatter_a_y.send(2)
+    pass_a(1)
+    pass_a(2)
     scatter_b_y.finish([7])
     scatter_a_z.finish([3])
 
@@ -501,7 +539,15 @@
         )
         wg_ref[:, columns_at] = source[y, near, :]
 
-    scatter_a_y.finish()
+    own_a = sa[y, pl.ds(z_rows(z), rb), :]
+    for index in (2, 0, 1):
+        slot = la_y.at[index]
+        pltpu.make_async_remote_copy(
+            src_ref=slot, dst_ref=slot, send_sem=ra_y_s.at[index], recv_sem=ra_y_r.at[index],
+            device_id=opposite, device_id_type=MESH,
+        ).wait_recv()
+        own_a = own_a + slot[...].astype(F32)
+    sa[y, pl.ds(z_rows(z), rb), :] = own_a
     restore(sa, 0, d.cols_a)
     scatter_b_z.finish()
     restore(sb, d.cols_a, d.cols_b)
@@ -547,18 +593,19 @@
         vm((2, t, depth), BF16), vm((2, ny, d.yrows, 2 * t), BF16),
         vm((2, t, hf), BF16), vm((2, t, hf), BF16), vm((2, t, hf), BF16),
         vm((d.pad, hf), BF16), vm((d.pad, hf), BF16),
+        vm((2 * t, d.cols_b), F32),
         vm((ny, d.yrows, d.cols_a), BF16), vm((ny, d.yrows, d.cols_b), BF16),
         vm((2 * t, d.cols_a), BF16), vm((2 * t, d.cols_b), BF16),
         vm((2, 2 * t, hf), BF16), vm((BLOCK, BLOCK), BF16),
         vm((ny, d.yrows, d.cols_a), F32), vm((ny, d.yrows, d.cols_b), F32),
         vm((ny, d.yrows, d.cols_a), BF16), vm((ny, d.yrows, d.cols_b), BF16),
-        vm((2, hz, ny, rb, d.cols_a), BF16), vm((2, hy, rb, d.cols_a), BF16),
+        vm((2, hz, ny, rb, d.cols_a), BF16), vm((3, rb, d.cols_a), BF16),
         vm((2, hy, nz, rb, d.cols_b), BF16), vm((2, hz, rb, d.cols_b), BF16),
         vm((8, t // 4, depth), F32), vm((4, t // 4, depth), BF16), vm((4, t // 4, depth), BF16),
         vm((3, t // 4, depth), BF16), vm((3, t // 4, depth), BF16),
-        sem(2, 5), sem(2, 2), sem(2, 3), sem(2, 2), sem(4 + d.blocks),
-        *pair(2, hy, 2), *pair(2, hz, ny), *pair(2, hz, 2), *pair(2, hy, nz),
-        *pair(2, hz, ny), *pair(2, hy, 2), *pair(2, hy, nz), *pair(2, hz, 2),
+        sem(2, 6), sem(2, 2), sem(2, 3), sem(2, 2), sem(4 + d.blocks),
+        *pair(3), *pair(2, hz, ny), *pair(2, hz, 2), *pair(2, hy, nz),
+        *pair(2, hz, ny), *pair(3), *pair(2, hy, nz), *pair(2, hz, 2),
     ]
     whole = pl.BlockSpec(memory_space=pltpu.VMEM)
     anywhere = pl.BlockSpec(memory_space=pl.ANY)

time: 90.2 us -> 87.7 us (0.972)
  Pallas kernels: 89.5 us -> 86.1 us
    pallas_call x1, Pallas kernels: 87.3 us -> 84 us  [local(): pl.pallas_call(functools.partial(kernel, d), out_shape=(jax.ShapeDtypeStr...]
where the time goes in v3:
time: 87.7 us; the launch traced here: 86.8 us
  Pallas kernels  86.1 us (98%)
    pallas_call x1, Pallas kernels, local(): pl.pallas_call(functools.partial(kernel, d), out_shape=(jax.ShapeDtypeStr...  84 us
    pallas_call x1, Pallas kernels, local(): pl.pallas_call(hand_over, out_shape=tuple((jax.ShapeDtypeStruct(r.shape,...  2.12 us

profile of v3, /device:TPU:8, one launch (start us, length us, event | category | flops | bytes accessed | tf_op | source)
XLA Modules:
  0.0 86.8 jit_solution(15544453039335246837)
XLA Ops:
  0.6 84.0 %gate_backward.1 = (bf16[32,2560]{1,0:T(8,128)(2,1)}, bf16[128,1792]{1,0:T(8,128)(2,1)}, f32[40,1792]{1,0:T(8,128)}) custom-call(bf16[128,2560]{1,0:T(8,128)(2,1)} %x_ref.1, bf16[40,1792]{1,0:T(8,128)(2,1)} %w_ref.1, bf16[128,1792]{1,0:T(8,128)(2,1)} %up_ref.1, bf16[128,1792]{1,0:T(8,128)(2,1)} %hg_ref.1, s32[1792]{0:T(1024)} %bits_ref.1, s32[14]{0:T(128)} %exp_ref.1), custom_call_target="tpu_custom_call" | custom-call | tf_op jit(solution)/shard_map/gate_backward/pallas_call | solution.py:612
  84.6 2.1 %hand_over.1 = (bf16[32,2560]{1,0:T(8,128)(2,1)}, bf16[128,1792]{1,0:T(8,128)(2,1)}, f32[40,1792]{1,0:T(8,128)}) custom-call(bf16[32,2560]{1,0:T(8,128)(2,1)} %get-tuple-element.6.a_ref, bf16[128,1792]{1,0:T(8,128)(2,1)} %get-tuple-element.7.b_ref, f32[40,1792]{1,0:T(8,128)} %get-tuple-element.8.c_ref), custom_call_target="tpu_custom_call" | custom-call | tf_op jit(solution)/shard_map/hand_over/pallas_call | solution.py:627

commit v4 on v3

--- a/solution.py
+++ b/solution.py
@@ -172,10 +172,10 @@
     dims,
     x_ref, w_ref, up_ref, hg_ref, bits_ref, exp_ref,
     ig_ref, ug_ref, wg_ref,
-    w_own, bits, x2, xt, hg2, up2, upg2, wsend, wrecv, early_b, wa, wb, g_a, g_b, turned, had,
+    w_own, bits, x2, xt, hg2, up2, upg2, wsend, wrecv, xz, early_a, early_b, wa, wb, g_a, g_b, turned, had,
     sa, sb, oa, ob, la_z, la_y, lb_y, lb_z,
-    part, core_out, core_in, chip_out, chip_in,
-    x_sems, core_sems, ip_sems, fin_sems, local_sems,
+    part, ig_own, core_out, core_in, chip_out, chip_in,
+    x_sems, core_sems, ip_sems, fin_sems, local_sems, store_sems,
     ga_y_s, ga_y_r, ga_z_s, ga_z_r, gb_z_s, gb_z_r, gb_y_s, gb_y_r,
     ra_z_s, ra_z_r, ra_y_s, ra_y_r, rb_y_s, rb_y_r, rb_z_s, rb_z_r,
 ):
@@ -208,6 +208,13 @@
         copy.start()
         loads.append(copy)
 
+    stores = []
+
+    def store(src, dst):
+        copy = pltpu.make_async_copy(src, dst, store_sems.at[len(stores)])
+        copy.start()
+        stores.append(copy)
+
     here = pl.ds(pl.multiple_of(xl * hf, BLOCK), hf)
     there = pl.ds(pl.multiple_of((1 - xl) * hf, BLOCK), hf)
 
@@ -295,6 +302,13 @@
         ).wait_recv()
 
     assemble(0, slice(d.cols_a, hf), d.cols_b, wb)
+    def turn_z(replica):
+        @pl.loop(0, d.nz)
+        def _(place):
+            tile = xt[replica, :, pl.ds(z_rows(place), rb), 0:t].reshape(d.ny * rb, t)
+            at = pl.ds(pl.multiple_of(replica * t, BLOCK), t)
+            xz[place, at, :] = tile.astype(F32).T.astype(BF16)
+
     gather_b_z.send(1)
     gather_b_y.send(1, [0])
     assemble(5, slice(0, d.cols_a), d.cols_a, wa)
@@ -328,6 +342,7 @@
     gather_a_z.send(2, [3])
     turn(xl, 3)
     gather_a_z.send(3, [0, 1])
+    turn_z(xl)
     theirs = x2.at[1 - xl, x_rows, :]
     landed(theirs, 1)
     sends.start(theirs, theirs, core_sems.at[0, 0], core_sems.at[1, 0], sibling)
@@ -347,6 +362,7 @@
     turn(1 - xl, 2)
     gather_b_y.send(2, [7])
     turn(1 - xl, 3)
+    turn_z(1 - xl)
     landed(hg2.at[1 - xl], 2)
     landed(up2.at[1 - xl], 3)
     for copy in loads[2:]:
@@ -365,9 +381,19 @@
     tiles_b = [(start, min(2 * BLOCK, d.cols_b - start)) for start in range(0, d.cols_b, 2 * BLOCK)]
     tiles_a = [(start, min(2 * BLOCK, d.cols_a - start)) for start in range(0, d.cols_a, 2 * BLOCK)]
     early = [ring_y.place(hops) for hops in (0, 1, -1)]
+    def gate_sum_z(columns, places):
+        total = 0.0
+        for place in places:
+            rows = wa[:, pl.ds(z_rows(place), rb), columns].reshape(d.ny * rb, columns.stop - columns.start)
+            total = total + jnp.dot(xz[place], rows, preferred_element_type=F32)
+        return total
+
+    for start, width in tiles_a:
+        columns = slice(start, start + width)
+        early_a[:, columns] = gate_sum_z(columns, [ring_z.place(hops) for hops in near_z[:-1]])
     for start, width in tiles_b:
         early_b[:, start : start + width] = gate_sum(wb, slice(start, start + width), early)
-    gather_b_y.finish()
+    gather_a_z.finish()
 
     def scale_of(block):
         return jnp.left_shift(1, exp_ref[xl * d.blocks + block]).astype(F32)
@@ -437,19 +463,21 @@
     )
     scatter_b_z = Scatter(ring_z, 2, along_z(sb), along_z(ob), at_rows(lb_z), (rb_z_s, rb_z_r), sends)
 
+    for start, width in tiles_a:
+        columns = slice(start, start + width)
+        gate = early_a[:, columns] + gate_sum_z(columns, [ring_z.place(near_z[-1])])
+        gate_tile(gate, g_a, 0, start, width)
+    grads_a(0, 1)
+    scatter_a_z.send(1)
+    gather_b_y.finish()
     for start, width in tiles_b:
         columns = slice(start, start + width)
         gate = early_b[:, columns] + gate_sum(wb, columns, [ring_y.place(2)])
         gate_tile(gate, g_b, d.cols_a, start, width)
     grads_b(0, 1)
     scatter_b_y.send(1)
-    gather_a_z.finish()
-    for start, width in tiles_a:
-        gate_tile(gate_sum(wa, slice(start, start + width), range(d.ny)), g_a, 0, start, width)
-    grads_a(0, 1)
-    scatter_a_z.send(1)
     sends.start(upg2.at[1 - xl], ug_ref.at[:, here], x_sems.at[0, 4], x_sems.at[1, 4], partner)
-    ug_ref[:, here] = upg2[xl]
+    store(upg2.at[xl], ug_ref.at[:, here])
     grads_a(1, 3)
     grads_b(1, 3)
     scatter_a_z.send(2)
@@ -517,6 +545,19 @@
     scatter_b_z.send(4)
     pass_a(1)
     pass_a(2)
+
+    mine = xl * 2 + xh
+    total = part[2 * mine + core] + core_in[mine].astype(F32)
+    for index in range(3):
+        slot = chip_in.at[index]
+        pltpu.make_async_remote_copy(
+            src_ref=slot, dst_ref=slot, send_sem=ip_sems.at[0, index], recv_sem=ip_sems.at[1, index],
+            device_id=across[index], device_id_type=MESH,
+        ).wait_recv()
+        total = total + slot[...].astype(F32)
+    ig_own[...] = total.astype(BF16)
+    store(ig_own, ig_ref)
+
     scatter_b_y.finish([7])
     scatter_a_z.finish([3])
 
@@ -537,7 +578,7 @@
         sends.start(
             source.at[y, far, :], wg_ref.at[:, columns_at], fin_sems.at[0, which], fin_sems.at[1, which], partner
         )
-        wg_ref[:, columns_at] = source[y, near, :]
+        store(source.at[y, near, :], wg_ref.at[:, columns_at])
 
     own_a = sa[y, pl.ds(z_rows(z), rb), :]
     for index in (2, 0, 1):
@@ -552,17 +593,6 @@
     scatter_b_z.finish()
     restore(sb, d.cols_a, d.cols_b)
 
-    mine = xl * 2 + xh
-    total = part[2 * mine + core] + core_in[mine].astype(F32)
-    for index in range(3):
-        slot = chip_in.at[index]
-        pltpu.make_async_remote_copy(
-            src_ref=slot, dst_ref=slot, send_sem=ip_sems.at[0, index], recv_sem=ip_sems.at[1, index],
-            device_id=across[index], device_id_type=MESH,
-        ).wait_recv()
-        total = total + slot[...].astype(F32)
-    ig_ref[...] = total.astype(BF16)
-
     landed(ug_ref.at[:, there], 4)
     for which, base, columns in ((0, 0, d.cols_a), (1, d.cols_a, d.cols_b)):
         slot = wg_ref.at[:, pl.ds(pl.multiple_of((1 - xl) * hf + base, BLOCK), columns)]
@@ -570,13 +600,24 @@
             src_ref=slot, dst_ref=slot, send_sem=fin_sems.at[0, which], recv_sem=fin_sems.at[1, which],
             device_id=partner, device_id_type=MESH,
         ).wait_recv()
+    for copy in stores:
+        copy.wait()
     sends.drain()
 
 
-def hand_over(a_ref, b_ref, c_ref, a_out, b_out, c_out):
-    a_out[...] = a_ref[...]
-    b_out[...] = b_ref[...]
-    c_out[...] = c_ref[...]
+def hand_over(a_ref, b_ref, c_ref, a_out, b_out, c_out, a_own, b_own, c_own, sems):
+    moves = []
+    for i, (src, own, dst) in enumerate(((c_ref, c_own, c_out), (a_ref, a_own, a_out), (b_ref, b_own, b_out))):
+        moves.append((
+            pltpu.make_async_copy(src, own, sems.at[0, i]), pltpu.make_async_copy(own, dst, sems.at[1, i])
+        ))
+    for into, _ in moves:
+        into.start()
+    for into, out in moves:
+        into.wait()
+        out.start()
+    for _, out in moves:
+        out.wait()
 
 
 def local(ny, nz, layer_input, gate_weight, up_value, hidden_grad, sign_bits, scale_exponent):
@@ -593,7 +634,7 @@
         vm((2, t, depth), BF16), vm((2, ny, d.yrows, 2 * t), BF16),
         vm((2, t, hf), BF16), vm((2, t, hf), BF16), vm((2, t, hf), BF16),
         vm((d.pad, hf), BF16), vm((d.pad, hf), BF16),
-        vm((2 * t, d.cols_b), F32),
+        vm((nz, 2 * t, ny * rb), BF16), vm((2 * t, d.cols_a), F32), vm((2 * t, d.cols_b), F32),
         vm((ny, d.yrows, d.cols_a), BF16), vm((ny, d.yrows, d.cols_b), BF16),
         vm((2 * t, d.cols_a), BF16), vm((2 * t, d.cols_b), BF16),
         vm((2, 2 * t, hf), BF16), vm((BLOCK, BLOCK), BF16),
@@ -601,13 +642,13 @@
         vm((ny, d.yrows, d.cols_a), BF16), vm((ny, d.yrows, d.cols_b), BF16),
         vm((2, hz, ny, rb, d.cols_a), BF16), vm((3, rb, d.cols_a), BF16),
         vm((2, hy, nz, rb, d.cols_b), BF16), vm((2, hz, rb, d.cols_b), BF16),
-        vm((8, t // 4, depth), F32), vm((4, t // 4, depth), BF16), vm((4, t // 4, depth), BF16),
+        vm((8, t // 4, depth), F32), vm((t // 4, depth), BF16), vm((4, t // 4, depth), BF16), vm((4, t // 4, depth), BF16),
         vm((3, t // 4, depth), BF16), vm((3, t // 4, depth), BF16),
-        sem(2, 6), sem(2, 2), sem(2, 3), sem(2, 2), sem(4 + d.blocks),
+        sem(2, 6), sem(2, 2), sem(2, 3), sem(2, 2), sem(4 + d.blocks), sem(4),
         *pair(3), *pair(2, hz, ny), *pair(2, hz, 2), *pair(2, hy, nz),
         *pair(2, hz, ny), *pair(3), *pair(2, hy, nz), *pair(2, hz, 2),
     ]
-    whole = pl.BlockSpec(memory_space=pltpu.VMEM)
+    hbm = pl.BlockSpec(memory_space=pltpu.HBM)
     anywhere = pl.BlockSpec(memory_space=pl.ANY)
     results = pl.pallas_call(
         functools.partial(kernel, d),
@@ -617,7 +658,7 @@
             jax.ShapeDtypeStruct((rows, hidden), F32),
         ),
         in_specs=[anywhere] * 5 + [pl.BlockSpec(memory_space=pltpu.SMEM)],
-        out_specs=(whole,) * 3,
+        out_specs=(hbm,) * 3,
         scratch_shapes=scratch,
         compiler_params=pltpu.CompilerParams(
             collective_id=0, has_side_effects=True, vmem_limit_bytes=56 * 1024 * 1024
@@ -627,8 +668,10 @@
     return pl.pallas_call(
         hand_over,
         out_shape=tuple(jax.ShapeDtypeStruct(r.shape, r.dtype) for r in results),
-        in_specs=[whole] * 3,
-        out_specs=(whole,) * 3,
+        in_specs=[hbm] * 3,
+        out_specs=(hbm,) * 3,
+        scratch_shapes=[*(vm(r.shape, r.dtype) for r in results), sem(2, 3)],
+        compiler_params=pltpu.CompilerParams(vmem_limit_bytes=60 * 1024 * 1024),
         name="hand_over",
     )(*results)
 

time: 87.7 us -> 85.4 us (0.974)
  Pallas kernels: 86.1 us -> 84.2 us
    pallas_call x1, Pallas kernels: 84 us -> 82.2 us  [local(): pl.pallas_call(functools.partial(kernel, d), out_shape=(jax.ShapeDtypeStr...]
where the time goes in v4:
time: 85.4 us; the launch traced here: 84.9 us
  Pallas kernels  84.2 us (99%)
    pallas_call x1, Pallas kernels, local(): pl.pallas_call(functools.partial(kernel, d), out_shape=(jax.ShapeDtypeStr...  82.2 us
    pallas_call x1, Pallas kernels, local(): pl.pallas_call(hand_over, out_shape=tuple((jax.ShapeDtypeStruct(r.shape,...  2 us

profile of v4, /device:TPU:8, one launch (start us, length us, event | category | flops | bytes accessed | tf_op | source)
XLA Modules:
  0.0 84.9 jit_solution(16885802135490834049)
XLA Ops:
  0.6 82.2 %gate_backward.1 = (bf16[32,2560]{1,0:T(8,128)(2,1)}, bf16[128,1792]{1,0:T(8,128)(2,1)}, f32[40,1792]{1,0:T(8,128)}) custom-call(bf16[128,2560]{1,0:T(8,128)(2,1)} %x_ref.1, bf16[40,1792]{1,0:T(8,128)(2,1)} %w_ref.1, bf16[128,1792]{1,0:T(8,128)(2,1)} %up_ref.1, bf16[128,1792]{1,0:T(8,128)(2,1)} %hg_ref.1, s32[1792]{0:T(1024)} %bits_ref.1, s32[14]{0:T(128)} %exp_ref.1), custom_call_target="tpu_custom_call" | custom-call | tf_op jit(solution)/shard_map/gate_backward/pallas_call | solution.py:653
  82.9 2.0 %hand_over.1 = (bf16[32,2560]{1,0:T(8,128)(2,1)}, bf16[128,1792]{1,0:T(8,128)(2,1)}, f32[40,1792]{1,0:T(8,128)}) custom-call(bf16[32,2560]{1,0:T(8,128)(2,1)} %get-tuple-element.6.a_ref, bf16[128,1792]{1,0:T(8,128)(2,1)} %get-tuple-element.7.b_ref, f32[40,1792]{1,0:T(8,128)} %get-tuple-element.8.c_ref), custom_call_target="tpu_custom_call" | custom-call | tf_op jit(solution)/shard_map/hand_over/pallas_call | solution.py:668

commit v5 on v4

--- a/solution.py
+++ b/solution.py
@@ -479,10 +479,7 @@
     sends.start(upg2.at[1 - xl], ug_ref.at[:, here], x_sems.at[0, 4], x_sems.at[1, 4], partner)
     store(upg2.at[xl], ug_ref.at[:, here])
     grads_a(1, 3)
-    grads_b(1, 3)
     scatter_a_z.send(2)
-    scatter_b_y.send(2, [0, 1, 2])
-
     def partial_tile(place):
         total = 0.0
         for w_part, g_part in ((wa, g_a), (wb, g_b)):
@@ -500,6 +497,9 @@
         core_out[q] = part[2 * q + 1 - core].astype(BF16)
 
     sends.start(core_out, core_in, core_sems.at[0, 1], core_sems.at[1, 1], sibling)
+
+    grads_b(1, 3)
+    scatter_b_y.send(2, [0, 1, 2])
 
     def x_stage():
         pltpu.make_async_remote_copy(

time: 85.4 us -> 84.1 us (0.985)
  Pallas kernels: 84.2 us -> 83.2 us
    pallas_call x1, Pallas kernels: 82.2 us -> 81.2 us  [local(): pl.pallas_call(functools.partial(kernel, d), out_shape=(jax.ShapeDtypeStr...]
where the time goes in v5:
time: 84.1 us; the launch traced here: 83.8 us
  Pallas kernels  83.2 us (99%)
    pallas_call x1, Pallas kernels, local(): pl.pallas_call(functools.partial(kernel, d), out_shape=(jax.ShapeDtypeStr...  81.2 us
    pallas_call x1, Pallas kernels, local(): pl.pallas_call(hand_over, out_shape=tuple((jax.ShapeDtypeStruct(r.shape,...  2 us

profile of v5, /device:TPU:8, one launch (start us, length us, event | category | flops | bytes accessed | tf_op | source)
XLA Modules:
  0.0 83.8 jit_solution(11309461484433057253)
XLA Ops:
  0.6 81.2 %gate_backward.1 = (bf16[32,2560]{1,0:T(8,128)(2,1)}, bf16[128,1792]{1,0:T(8,128)(2,1)}, f32[40,1792]{1,0:T(8,128)}) custom-call(bf16[128,2560]{1,0:T(8,128)(2,1)} %x_ref.1, bf16[40,1792]{1,0:T(8,128)(2,1)} %w_ref.1, bf16[128,1792]{1,0:T(8,128)(2,1)} %up_ref.1, bf16[128,1792]{1,0:T(8,128)(2,1)} %hg_ref.1, s32[1792]{0:T(1024)} %bits_ref.1, s32[14]{0:T(128)} %exp_ref.1), custom_call_target="tpu_custom_call" | custom-call | tf_op jit(solution)/shard_map/gate_backward/pallas_call | solution.py:653
  81.8 2.0 %hand_over.1 = (bf16[32,2560]{1,0:T(8,128)(2,1)}, bf16[128,1792]{1,0:T(8,128)(2,1)}, f32[40,1792]{1,0:T(8,128)}) custom-call(bf16[32,2560]{1,0:T(8,128)(2,1)} %get-tuple-element.6.a_ref, bf16[128,1792]{1,0:T(8,128)(2,1)} %get-tuple-element.7.b_ref, f32[40,1792]{1,0:T(8,128)} %get-tuple-element.8.c_ref), custom_call_target="tpu_custom_call" | custom-call | tf_op jit(solution)/shard_map/hand_over/pallas_call | solution.py:668
